TPU v7x, 32 devices: a whole 2x2x4 slice. The times are simulated.
32 devices in a mesh: grp: 4 (over z), box: 8 (over y, x, core).
Axes of the slice: x: 2, y: 2, z: 4, core: 2. Of those that a mesh axis runs over, the one named last changes fastest.
Arguments:
- weights: bfloat16 [4096, 8192], P(('grp', 'box')), may hold values from -6 to 6
- tables: bfloat16 [32, 2, 64, 64], replicated, may hold values from -0.5 to 0.5
- pattern: int32 [4096, 4], P(('grp', 'box')), may hold values from 0 to 31
- partner_slot: int32 [4096, 4], P(('grp', 'box')), may hold values from 0 to 127, as said below
- target_order: int32 [32, 128], P(('grp', 'box')), may hold values from 0 to 127, each once within a row
Outputs:
- targets: bfloat16 [4096, 8192], P(('grp', 'box'))
Inputs may be any that keep to these rules, and one draw needn't show every extreme that they name: For each device and level, partner_slot over that device's boxes is a permutation of its positions; at the last level, 3, partner_slot[n, l] lies in the same block of 128 // 4 positions as n's own position.
All inputs are finite; a program needn't handle non-finite values.
Results may differ from a plain program's by a relative error of at most 0.0064.
Values may be sent and summed in bfloat16 or wider, within the bound.
A program may use at most 64 MiB of HBM per device.

v0:
```python
import functools

import jax
import jax.numpy as jnp
from jax import lax
from jax.experimental import pallas as pl
from jax.experimental.pallas import tpu as pltpu
from jax.sharding import PartitionSpec as P

MESH = pl.DeviceIdType.MESH
COLS = 16
UNROLL = 4


def pick(ref, code_a, code_b, low_lanes):
    a = ref[code_a // 2]
    b = ref[code_b // 2]
    a = jnp.where(code_a % 2 == 1, pltpu.roll(a, 64, 1), a)
    b = jnp.where(code_b % 2 == 1, b, pltpu.roll(b, 64, 1))
    return jnp.where(low_lanes, a, b)


def kernel(groups, boxes, chunks, pairs, x_ref, tbl_ref, pat_ref, slot_ref, order_ref, meta_ref, out_ref, *scratch):
    it = iter(scratch)
    recv = [[next(it) for _ in range(chunks)] for _ in range(3)]
    made = [[next(it) for _ in range(chunks)] for _ in range(3)]
    zbuf = [next(it) for _ in range(chunks)]
    meta_recv, meta_smem, par_s, pat_s = (next(it) for _ in range(4))
    send_sem, recv_sem, zsend_sem, zrecv_sem, zown_sem, msend_sem, mrecv_sem, mown_sem = it

    n_box = 2 * pairs
    piece = n_box // groups
    ppiece = pairs // groups
    grp = lax.axis_index("grp")
    box = lax.axis_index("box")
    box_bits = boxes.bit_length() - 1
    partners = []
    for level in range(3):
        flip = 1 << (box_bits - 3 + level)
        bit = (box // flip) % 2
        partners.append(box + flip - 2 * flip * bit)

    barrier = pltpu.get_barrier_semaphore()
    for other in partners:
        pl.semaphore_signal(barrier, inc=1, device_id={"box": other}, device_id_type=MESH)
    for off in range(1, groups):
        pl.semaphore_signal(barrier, inc=1, device_id={"grp": (grp + off) % groups}, device_id_type=MESH)
    pl.semaphore_wait(barrier, 3 + groups - 1)

    def level_copy(level, c):
        src = x_ref.at[c] if level == 0 else made[level - 1][c]
        return pltpu.make_async_remote_copy(
            src_ref=src,
            dst_ref=recv[level][c],
            send_sem=send_sem.at[level, c],
            recv_sem=recv_sem.at[level, c],
            device_id={"box": partners[level]},
            device_id_type=MESH,
        )

    def z_copy(c, off):
        to = (grp + off) % groups
        return pltpu.make_async_remote_copy(
            src_ref=made[2][c].at[pl.ds(to * ppiece, ppiece)],
            dst_ref=zbuf[c].at[pl.ds(grp * ppiece, ppiece)],
            send_sem=zsend_sem.at[c, off - 1],
            recv_sem=zrecv_sem.at[c, off - 1],
            device_id={"grp": to},
            device_id_type=MESH,
        )

    def z_own(c):
        mine = pl.ds(grp * ppiece, ppiece)
        return pltpu.make_async_copy(made[2][c].at[mine], zbuf[c].at[mine], zown_sem.at[c])

    def meta_copy(off):
        to = (grp + off) % groups
        return pltpu.make_async_remote_copy(
            src_ref=meta_ref.at[to],
            dst_ref=meta_recv.at[grp],
            send_sem=msend_sem.at[off - 1],
            recv_sem=mrecv_sem.at[off - 1],
            device_id={"grp": to},
            device_id_type=MESH,
        )

    for c in range(chunks):
        level_copy(0, c).start()
    for off in range(1, groups):
        meta_copy(off).start()
    pltpu.make_async_copy(meta_ref.at[grp], meta_recv.at[grp], mown_sem.at[0]).start()

    low_lanes = lax.broadcasted_iota(jnp.int32, (COLS, 128), 1) < 64

    def combine(own, other, pa, pb):
        left = jnp.concatenate([own, other], axis=1)
        right = jnp.concatenate(
            [tbl_ref[0, pa, 0], tbl_ref[1, pb, 0], tbl_ref[0, pa, 1], tbl_ref[1, pb, 1]], axis=0
        )
        return jnp.dot(left, right, preferred_element_type=jnp.float32).astype(jnp.bfloat16)

    def compute(level, c):
        level_copy(level, c).wait_recv()
        src = x_ref.at[c] if level == 0 else made[level - 1][c]

        @pl.loop(0, pairs // UNROLL)
        def _(i):
            for u in range(UNROLL):
                j = i * UNROLL + u
                at = level * n_box + 2 * j
                other = pick(recv[level][c], slot_ref[at], slot_ref[at + 1], low_lanes)
                made[level][c][j] = combine(src[j], other, pat_ref[at], pat_ref[at + 1])

        if level < 2:
            level_copy(level + 1, c).start()
        else:
            for off in range(1, groups):
                z_copy(c, off).start()
            z_own(c).start()

    def prepare_last():
        for off in range(1, groups):
            meta_copy(off).wait_recv()
        pltpu.make_async_copy(meta_ref.at[grp], meta_recv.at[grp], mown_sem.at[0]).wait()
        copy = pltpu.make_async_copy(meta_recv, meta_smem, mown_sem.at[1])
        copy.start()
        copy.wait()

        @pl.loop(0, n_box)
        def _(q):
            z = order_ref[q]
            h = z // piece
            s = z % piece
            par_s[q] = (h + 1 - 2 * (h % 2)) * piece + meta_smem[h, 1, s]
            pat_s[q] = meta_smem[h, 0, s]

    def last(c):
        for off in range(1, groups):
            z_copy(c, off).wait_recv()
        z_own(c).wait()

        @pl.loop(0, pairs // UNROLL)
        def _(i):
            for u in range(UNROLL):
                j = i * UNROLL + u
                own = pick(zbuf[c], order_ref[2 * j], order_ref[2 * j + 1], low_lanes)
                other = pick(zbuf[c], par_s[2 * j], par_s[2 * j + 1], low_lanes)
                out_ref[c, j] = combine(own, other, pat_s[2 * j], pat_s[2 * j + 1])

    for c in range(chunks):
        compute(0, c)
    prepare_last()
    for t in range(chunks + 2):
        for level in (1, 2, 3):
            c = t - (level - 1)
            if 0 <= c < chunks:
                if level < 3:
                    compute(level, c)
                else:
                    last(c)

    for c in range(chunks):
        for level in range(3):
            level_copy(level, c).wait_send()
        for off in range(1, groups):
            z_copy(c, off).wait_send()
    for off in range(1, groups):
        meta_copy(off).wait_send()


def body(weights, tables, pattern, partner_slot, target_order):
    n_box, width = weights.shape
    kinds, _, rank, _ = tables.shape
    nrhs = width // rank
    chunks = nrhs // COLS
    pairs = n_box // 2
    groups = lax.axis_size("grp")
    boxes = lax.axis_size("box")
    piece = n_box // groups

    with jax.named_scope("pack_weights"):
        x = weights.reshape(pairs, 2, rank, chunks, COLS)
        x = jnp.transpose(x, (3, 0, 4, 1, 2)).reshape(chunks, pairs, COLS, 2 * rank)
    with jax.named_scope("pack_tables"):
        turned = jnp.swapaxes(tables, 2, 3)
        zero = jnp.zeros_like(turned)
        tbl = jnp.stack([jnp.concatenate([turned, zero], 3), jnp.concatenate([zero, turned], 3)])
    pat = jnp.transpose(pattern[:, :3]).reshape(-1)
    slot = jnp.transpose(partner_slot[:, :3]).reshape(-1)
    meta = jnp.stack([pattern[:, 3].reshape(groups, piece), partner_slot[:, 3].reshape(groups, piece) % piece], 1)
    meta = jnp.pad(meta, ((0, 0), (0, 6), (0, 128 - piece)))

    block = (pairs, COLS, 2 * rank)
    vmem = pl.BlockSpec(memory_space=pltpu.VMEM)
    smem = pl.BlockSpec(memory_space=pltpu.SMEM)
    dma = pltpu.SemaphoreType.DMA
    out = pl.pallas_call(
        functools.partial(kernel, groups, boxes, chunks, pairs),
        out_shape=jax.ShapeDtypeStruct((chunks,) + block, jnp.bfloat16),
        in_specs=[vmem, vmem, smem, smem, smem, vmem],
        out_specs=vmem,
        scratch_shapes=[pltpu.VMEM(block, jnp.bfloat16)] * (7 * chunks)
        + [
            pltpu.VMEM((groups, 8, 128), jnp.int32),
            pltpu.SMEM((groups, 8, 128), jnp.int32),
            pltpu.SMEM((n_box,), jnp.int32),
            pltpu.SMEM((n_box,), jnp.int32),
            dma((3, chunks)),
            dma((3, chunks)),
            dma((chunks, groups - 1)),
            dma((chunks, groups - 1)),
            dma((chunks,)),
            dma((groups - 1,)),
            dma((groups - 1,)),
            dma((2,)),
        ],
        compiler_params=pltpu.CompilerParams(
            collective_id=0, has_side_effects=True, vmem_limit_bytes=40 * 1024 * 1024
        ),
        cost_estimate=pl.CostEstimate(flops=4 * 2 * n_box * rank * 2 * rank * nrhs, bytes_accessed=4 * n_box * width, transcendentals=0),
    )(x, tbl, pat, slot, target_order[0], meta)

    with jax.named_scope("unpack_targets"):
        out = out.reshape(chunks, pairs, COLS, 2, rank)
        return jnp.transpose(out, (1, 3, 4, 0, 2)).reshape(n_box, width)


def solution(mesh):
    placed = (
        P(("grp", "box"), None),
        P(),
        P(("grp", "box"), None),
        P(("grp", "box"), None),
        P(("grp", "box"), None),
    )
    return jax.shard_map(
        body, mesh=mesh, in_specs=placed, out_specs=P(("grp", "box"), None), check_vma=False
    )
```

profile of v0, /device:TPU:0, one launch (start us, length us, event | category | flops | bytes accessed | tf_op | source)
XLA Modules:
  0.0 220.8 jit_solution(10972507857275092154)
XLA Ops:
  0.0 16.8 %reshape.70 = bf16[64,2,64,8,16]{4,3,2,1,0:T(8,128)(2,1)} reshape(bf16[128,8192]{1,0:T(8,128)(2,1)} %param.5) | data formatting | bytes 4194304 | tf_op jit(solution)/shard_map/pack_weights/reshape | solution.py:182
  16.8 14.6 %copy.20.x_ref = bf16[8,64,16,128]{3,2,1,0:T(8,128)(2,1)S(1)} copy(bf16[8,64,16,128]{2,0,3,1:T(8,128)(2,1)} %bitcast.26) | data formatting | bytes 4194304 | tf_op jit(solution)/shard_map/pack_weights/reshape | solution.py:183
  31.4 1.6 copy.14
  33.0 0.6 pad_bitcast_fusion.1
  33.6 0.0 copy-start.3
  33.6 0.0 copy-start.4
  33.6 0.0 copy-start.2
  33.7 1.5 pad_maximum_fusion.tbl_ref
  35.2 0.0 copy-done.3
  35.2 0.0 copy-done.4
  35.2 0.1 reshape_squeeze.3
  35.3 0.1 stack_reshape_squeeze.3
  35.4 0.0 copy-done.2
  35.4 0.0 copy-start.1
  35.4 1.6 copy-done.1
  37.0 139.5 %shard_map.55 = bf16[8,64,16,128]{3,2,1,0:T(8,128)(2,1)S(1)} custom-call(bf16[8,64,16,128]{3,2,1,0:T(8,128)(2,1)S(1)} %copy.20.x_ref, bf16[2,32,2,64,128]{4,3,2,1,0:T(8,128)(2,1)S(1)} %copy-done.1, s32[384]{0:T(512)S(1)} %get-tuple-element.10.pat_ref, s32[384]{0:T(512)S(1)} %get-tuple-element.9.slot_ref, s32[128]{0:T(128)S(1)} %bitcast.24, ...), custom_call_target="tpu_custom_call" | custom-call | flops 1073741824 | bytes 4194304 | tf_op jit(solution)/shard_map/pallas_call | solution.py:197
  176.5 0.0 copy-start
  176.6 1.3 copy-done
  177.9 13.2 %copy.21 = bf16[8,64,16,128]{2,0,3,1:T(8,128)(2,1)} copy(bf16[8,64,16,128]{3,2,1,0:T(8,128)(2,1)} %copy-done) | data formatting | bytes 4194304 | tf_op jit(solution)/shard_map/unpack_targets/reshape | solution.py:224
  191.1 29.7 %reshape.75 = bf16[128,8192]{1,0:T(8,128)(2,1)} reshape(bf16[64,2,64,8,16]{4,3,2,1,0:T(8,128)(2,1)} %bitcast.25) | data formatting | bytes 4194304 | tf_op jit(solution)/shard_map/unpack_targets/reshape | solution.py:225
  (5 shorter events, 0.1 us)
Async XLA Ops:
  33.6 1.5 copy-start.3
  33.6 1.5 copy-start.4
  33.6 1.7 copy-start.2
  35.4 1.6 copy-start.1
  176.5 1.3 copy-start
where the time goes:
time: 222 us; the launch traced here: 221 us
  Pallas kernels  140 us (63%)
  local copies, waits for them, and re-layouts  79.7 us (36%)
    pallas_call x1, Pallas kernels, body(): pl.pallas_call(functools.partial(kernel, groups, boxes, chunks, pairs), o...  140 us
    reshape x1, local copies, waits for them, and re-layouts, body(): return jnp.transpose(out, (1, 3, 4, 0, 2)).reshape(n_box, width)  29.7 us
    reshape x1, local copies, waits for them, and re-layouts, body(): x = weights.reshape(pairs, 2, rank, chunks, COLS)  16.8 us
    reshape x1, local copies, waits for them, and re-layouts, body(): x = jnp.transpose(x, (3, 0, 4, 1, 2)).reshape(chunks, pairs, COLS, 2 * rank)  14.6 us
    reshape x1, local copies, waits for them, and re-layouts, body(): out = out.reshape(chunks, pairs, COLS, 2, rank)  13.2 us
    unnamed x11, local copies, waits for them, and re-layouts  4.53 us

commit v1 on v0

--- a/solution.py
+++ b/solution.py
@@ -168,6 +168,53 @@
         meta_copy(off).wait_send()
 
 
+def pack_kernel(w_ref, x_ref):
+    chunks = x_ref.shape[0]
+    rank = w_ref.shape[1] // 128
+    w = jnp.stack([w_ref[:, a * 128 : (a + 1) * 128].astype(jnp.float32) for a in range(rank)])
+    w = jnp.transpose(w, (1, 0, 2))
+    for i in range(w.shape[0] // 2):
+        turned = jnp.transpose(w[2 * i : 2 * i + 2].reshape(2 * rank, 128))
+        x_ref[:, i] = turned.astype(jnp.bfloat16).reshape(chunks, COLS, 2 * rank)
+
+
+def unpack_kernel(y_ref, o_ref):
+    rank = o_ref.shape[1] // 128
+    boxes = []
+    for i in range(y_ref.shape[1]):
+        y = y_ref[:, i].reshape(128, 2 * rank).astype(jnp.float32)
+        boxes.append(jnp.transpose(y).reshape(2, rank, 128))
+    o = jnp.transpose(jnp.concatenate(boxes, axis=0), (1, 0, 2))
+    for a in range(rank):
+        o_ref[:, a * 128 : (a + 1) * 128] = o[a].astype(jnp.bfloat16)
+
+
+def pack(w, rank):
+    n_box, width = w.shape
+    chunks = width // rank // COLS
+    return pl.pallas_call(
+        pack_kernel,
+        out_shape=jax.ShapeDtypeStruct((chunks, n_box // 2, COLS, 2 * rank), w.dtype),
+        grid=(n_box // 16,),
+        in_specs=[pl.BlockSpec((16, width), lambda i: (i, 0))],
+        out_specs=pl.BlockSpec((chunks, 8, COLS, 2 * rank), lambda i: (0, i, 0, 0)),
+        compiler_params=pltpu.CompilerParams(vmem_limit_bytes=32 * 1024 * 1024),
+    )(w)
+
+
+def unpack(y, rank):
+    chunks, pairs = y.shape[:2]
+    width = rank * chunks * COLS
+    return pl.pallas_call(
+        unpack_kernel,
+        out_shape=jax.ShapeDtypeStruct((2 * pairs, width), y.dtype),
+        grid=(pairs // 8,),
+        in_specs=[pl.BlockSpec((chunks, 8, COLS, 2 * rank), lambda i: (0, i, 0, 0))],
+        out_specs=pl.BlockSpec((16, width), lambda i: (i, 0)),
+        compiler_params=pltpu.CompilerParams(vmem_limit_bytes=32 * 1024 * 1024),
+    )(y)
+
+
 def body(weights, tables, pattern, partner_slot, target_order):
     n_box, width = weights.shape
     kinds, _, rank, _ = tables.shape
@@ -179,8 +226,7 @@
     piece = n_box // groups
 
     with jax.named_scope("pack_weights"):
-        x = weights.reshape(pairs, 2, rank, chunks, COLS)
-        x = jnp.transpose(x, (3, 0, 4, 1, 2)).reshape(chunks, pairs, COLS, 2 * rank)
+        x = pack(weights, rank)
     with jax.named_scope("pack_tables"):
         turned = jnp.swapaxes(tables, 2, 3)
         zero = jnp.zeros_like(turned)
@@ -221,8 +267,7 @@
     )(x, tbl, pat, slot, target_order[0], meta)
 
     with jax.named_scope("unpack_targets"):
-        out = out.reshape(chunks, pairs, COLS, 2, rank)
-        return jnp.transpose(out, (1, 3, 4, 0, 2)).reshape(n_box, width)
+        return unpack(out, rank)
 
 
 def solution(mesh):

time: 222 us -> 151 us (0.68)
  local copies, waits for them, and re-layouts: 79.7 us -> 5.2 us
  Pallas kernels: 140 us -> 145 us
    reshape x4 -> x0, local copies, waits for them, and re-layouts: 74.3 us -> none  [the longest x1 29.7 us: body(): return jnp.transpose(out, (1, 3, 4, 0, 2)).reshape(n_box, width)]
    pallas_call x0 -> x2, Pallas kernels: none -> 5.57 us  [the longest x1 3.88 us: unpack(): pl.pallas_call(unpack_kernel, out_shape=jax.ShapeDtypeStruct((2 * pairs,...]
    unnamed x11 -> x5, local copies, waits for them, and re-layouts: 4.53 us -> 2.99 us
where the time goes in v1:
time: 151 us
  Pallas kernels  145 us (96%)
  local copies, waits for them, and re-layouts  5.2 us (3%)
    pallas_call x1, Pallas kernels, body(): pl.pallas_call(functools.partial(kernel, groups, boxes, chunks, pairs), o...  140 us
    pallas_call x1, Pallas kernels, unpack(): pl.pallas_call(unpack_kernel, out_shape=jax.ShapeDtypeStruct((2 * pairs,...  3.88 us

profile of v1, /device:TPU:0, one launch (start us, length us, event | category | flops | bytes accessed | tf_op | source)
XLA Modules:
  0.0 150.6 jit_solution(8928280551021421597)
XLA Ops:
  0.0 0.7 slice_reduce_fusion
  0.7 0.1 reshape_squeeze.3
  0.8 0.1 stack_reshape_squeeze.3
  0.9 0.7 slice_bitcast_fusion
  1.6 1.6 %copy.6 = bf16[32,2,64,64]{2,3,1,0:T(8,128)(2,1)S(1)} copy(bf16[32,2,64,64]{3,2,1,0:T(8,128)(2,1)} %param.6) | data formatting | bytes 1048576 | tf_op args[1]
  3.2 0.6 pad_bitcast_fusion.1
  3.9 0.0 copy-start
  3.9 0.2 pad_maximum_fusion.tbl_ref
  4.1 1.4 copy-done
  5.5 0.0 copy-start.1
  5.5 1.7 %pack_weights.1.x_ref = bf16[8,64,16,128]{3,2,1,0:T(8,128)(2,1)S(1)} custom-call(bf16[128,8192]{1,0:T(8,128)(2,1)S(1)} %copy-done), custom_call_target="tpu_custom_call" | custom-call | tf_op jit(solution)/shard_map/pack_weights/pallas_call | solution.py:195
  7.2 0.0 copy-done.1
  7.2 139.6 %shard_map.55.y_ref = bf16[8,64,16,128]{3,2,1,0:T(8,128)(2,1)S(1)} custom-call(bf16[8,64,16,128]{3,2,1,0:T(8,128)(2,1)S(1)} %pack_weights.1.x_ref, bf16[2,32,2,64,128]{4,3,2,1,0:T(8,128)(2,1)S(1)} %pad_maximum_fusion.tbl_ref, s32[384]{0:T(512)S(1)} %get-tuple-element.10.pat_ref, s32[384]{0:T(512)S(1)} %get-tuple-element.9.slot_ref, s32[128]{0:T(128)S(1)} %bitcast.16, ...), custom_call_target="tpu_custom_call" | custom-call | flops 1073741824 | bytes 4194304 | tf_op jit(solution)/shard_map/pallas_call | solution.py:243
  146.7 3.9 %unpack_targets.1 = bf16[128,8192]{1,0:T(8,128)(2,1)} custom-call(bf16[8,64,16,128]{3,2,1,0:T(8,128)(2,1)S(1)} %shard_map.55.y_ref), custom_call_target="tpu_custom_call" | custom-call | tf_op jit(solution)/shard_map/unpack_targets/pallas_call | solution.py:208
  (3 shorter events, 0.0 us)
Async XLA Ops:
  3.9 1.6 %copy-start = (bf16[128,8192]{1,0:T(8,128)(2,1)S(1)}, bf16[128,8192]{1,0:T(8,128)(2,1)}, u32[]{:S(2)}) copy-start(bf16[128,8192]{1,0:T(8,128)(2,1)} %w_ref.1) | copy-start | bytes 6291460
  5.5 1.7 %copy-start.1 = (s32[1,128]{1,0:T(1,128)S(1)}, s32[1,128]{1,0:T(1,128)}, u32[]{:S(2)}) copy-start(s32[1,128]{1,0:T(1,128)} %param.9) | copy-start | bytes 1540

commit v2 on v1

--- a/solution.py
+++ b/solution.py
@@ -9,14 +9,14 @@
 
 MESH = pl.DeviceIdType.MESH
 COLS = 16
-UNROLL = 4
-
-
-def pick(ref, code_a, code_b, low_lanes):
-    a = ref[code_a // 2]
-    b = ref[code_b // 2]
-    a = jnp.where(code_a % 2 == 1, pltpu.roll(a, 64, 1), a)
-    b = jnp.where(code_b % 2 == 1, b, pltpu.roll(b, 64, 1))
+UNROLL = 32
+
+
+def pick(ref, code_low, code_high, low_lanes):
+    a = ref[code_low >> 1]
+    b = ref[code_high >> 1]
+    a = pltpu.roll(a, (code_low & 1) * 64, 1)
+    b = pltpu.roll(b, 64 - (code_high & 1) * 64, 1)
     return jnp.where(low_lanes, a, b)
 
 
@@ -92,12 +92,13 @@
 
     low_lanes = lax.broadcasted_iota(jnp.int32, (COLS, 128), 1) < 64
 
+    low_table = lax.broadcasted_iota(jnp.int32, (128, 128), 1) < 64
+
     def combine(own, other, pa, pb):
-        left = jnp.concatenate([own, other], axis=1)
-        right = jnp.concatenate(
-            [tbl_ref[0, pa, 0], tbl_ref[1, pb, 0], tbl_ref[0, pa, 1], tbl_ref[1, pb, 1]], axis=0
-        )
-        return jnp.dot(left, right, preferred_element_type=jnp.float32).astype(jnp.bfloat16)
+        left = jnp.concatenate([jnp.where(low_lanes, own, other), jnp.where(low_lanes, other, own)], axis=0)
+        right = jnp.where(low_table, tbl_ref[pa], tbl_ref[pb])
+        both = jnp.dot(left, right, preferred_element_type=jnp.float32)
+        return jnp.where(low_lanes, both[:COLS], both[COLS:]).astype(jnp.bfloat16)
 
     def compute(level, c):
         level_copy(level, c).wait_recv()
@@ -105,11 +106,14 @@
 
         @pl.loop(0, pairs // UNROLL)
         def _(i):
+            done = []
             for u in range(UNROLL):
                 j = i * UNROLL + u
                 at = level * n_box + 2 * j
-                other = pick(recv[level][c], slot_ref[at], slot_ref[at + 1], low_lanes)
-                made[level][c][j] = combine(src[j], other, pat_ref[at], pat_ref[at + 1])
+                other = pick(recv[level][c], slot_ref[at + 1], slot_ref[at], low_lanes)
+                done.append(combine(src[j], other, pat_ref[at], pat_ref[at + 1]))
+            for u in range(UNROLL):
+                made[level][c][i * UNROLL + u] = done[u]
 
         if level < 2:
             level_copy(level + 1, c).start()
@@ -141,11 +145,14 @@
 
         @pl.loop(0, pairs // UNROLL)
         def _(i):
+            done = []
             for u in range(UNROLL):
                 j = i * UNROLL + u
                 own = pick(zbuf[c], order_ref[2 * j], order_ref[2 * j + 1], low_lanes)
-                other = pick(zbuf[c], par_s[2 * j], par_s[2 * j + 1], low_lanes)
-                out_ref[c, j] = combine(own, other, pat_s[2 * j], pat_s[2 * j + 1])
+                other = pick(zbuf[c], par_s[2 * j + 1], par_s[2 * j], low_lanes)
+                done.append(combine(own, other, pat_s[2 * j], pat_s[2 * j + 1]))
+            for u in range(UNROLL):
+                out_ref[c, i * UNROLL + u] = done[u]
 
     for c in range(chunks):
         compute(0, c)
@@ -229,8 +236,8 @@
         x = pack(weights, rank)
     with jax.named_scope("pack_tables"):
         turned = jnp.swapaxes(tables, 2, 3)
-        zero = jnp.zeros_like(turned)
-        tbl = jnp.stack([jnp.concatenate([turned, zero], 3), jnp.concatenate([zero, turned], 3)])
+        first, second = turned[:, 0], turned[:, 1]
+        tbl = jnp.concatenate([jnp.concatenate([first, second], 1), jnp.concatenate([second, first], 1)], 2)
     pat = jnp.transpose(pattern[:, :3]).reshape(-1)
     slot = jnp.transpose(partner_slot[:, :3]).reshape(-1)
     meta = jnp.stack([pattern[:, 3].reshape(groups, piece), partner_slot[:, 3].reshape(groups, piece) % piece], 1)

time: 151 us -> 86.4 us (0.57)
  Pallas kernels: 145 us -> 81.3 us
    pallas_call x1, Pallas kernels: 140 us -> 75.7 us  [body(): pl.pallas_call(functools.partial(kernel, groups, boxes, chunks, pairs), o...]
where the time goes in v2:
time: 86.4 us; the launch traced here: 86.2 us
  Pallas kernels  81.3 us (94%)
  local copies, waits for them, and re-layouts  4.2 us (5%)
    pallas_call x1, Pallas kernels, body(): pl.pallas_call(functools.partial(kernel, groups, boxes, chunks, pairs), o...  75.7 us
    pallas_call x1, Pallas kernels, unpack(): pl.pallas_call(unpack_kernel, out_shape=jax.ShapeDtypeStruct((2 * pairs,...  3.88 us
    unnamed x5, local copies, waits for them, and re-layouts  2.54 us

profile of v2, /device:TPU:0, one launch (start us, length us, event | category | flops | bytes accessed | tf_op | source)
XLA Modules:
  0.0 86.2 jit_solution(1439192431451807806)
XLA Ops:
  0.0 0.7 slice_reduce_fusion
  0.7 0.1 reshape_squeeze.3
  0.8 0.1 stack_reshape_squeeze.3
  0.9 0.7 slice_bitcast_fusion.2
  1.6 1.6 %copy.6 = bf16[32,2,64,64]{2,3,0,1:T(8,128)(2,1)S(1)} copy(bf16[32,2,64,64]{3,2,1,0:T(8,128)(2,1)} %param.6) | data formatting | bytes 1048576 | tf_op args[1]
  3.2 0.0 copy-start
  3.3 0.1 slice_bitcast_fusion
  3.3 0.6 maximum_maximum_fusion.tbl_ref
  3.9 0.9 %copy-done = bf16[128,8192]{1,0:T(8,128)(2,1)S(1)} copy-done((bf16[128,8192]{1,0:T(8,128)(2,1)S(1)}, bf16[128,8192]{1,0:T(8,128)(2,1)}, u32[]{:S(2)}) %copy-start) | copy-done | bytes 2097176
  4.8 0.0 copy-start.1
  4.8 1.7 %pack_weights.1.x_ref = bf16[8,64,16,128]{3,2,1,0:T(8,128)(2,1)S(1)} custom-call(bf16[128,8192]{1,0:T(8,128)(2,1)S(1)} %copy-done), custom_call_target="tpu_custom_call" | custom-call | tf_op jit(solution)/shard_map/pack_weights/pallas_call | solution.py:202
  6.5 0.0 copy-done.1
  6.5 75.7 %shard_map.55.y_ref = bf16[8,64,16,128]{3,2,1,0:T(8,128)(2,1)S(1)} custom-call(bf16[8,64,16,128]{3,2,1,0:T(8,128)(2,1)S(1)} %pack_weights.1.x_ref, bf16[32,128,128]{2,1,0:T(8,128)(2,1)S(1)} %maximum_maximum_fusion.tbl_ref, s32[384]{0:T(512)S(1)} %get-tuple-element.10.pat_ref, s32[384]{0:T(512)S(1)} %get-tuple-element.9.slot_ref, s32[128]{0:T(128)S(1)} %bitcast.16, ...), custom_call_target="tpu_custom_call" | custom-call | flops 1073741824 | bytes 4194304 | tf_op jit(solution)/shard_map/pallas_call | solution.py:250
  82.3 3.9 %unpack_targets.1 = bf16[128,8192]{1,0:T(8,128)(2,1)} custom-call(bf16[8,64,16,128]{3,2,1,0:T(8,128)(2,1)S(1)} %shard_map.55.y_ref), custom_call_target="tpu_custom_call" | custom-call | tf_op jit(solution)/shard_map/unpack_targets/pallas_call | solution.py:215
  (3 shorter events, 0.0 us)
Async XLA Ops:
  3.2 1.6 %copy-start = (bf16[128,8192]{1,0:T(8,128)(2,1)S(1)}, bf16[128,8192]{1,0:T(8,128)(2,1)}, u32[]{:S(2)}) copy-start(bf16[128,8192]{1,0:T(8,128)(2,1)} %w_ref.1) | copy-start | bytes 6291460
  4.8 1.7 %copy-start.1 = (s32[1,128]{1,0:T(1,128)S(1)}, s32[1,128]{1,0:T(1,128)}, u32[]{:S(2)}) copy-start(s32[1,128]{1,0:T(1,128)} %param.9) | copy-start | bytes 1540
